TPU v7x, 512 devices: a whole 4x8x8 slice. The times are simulated.
512 devices in a mesh: chan: 64 (over y_hi, z, core), win: 8 (over x, y_lo).
Axes of the slice: x: 4, y: 8 (y_hi: 4, y_lo: 2; y = y_hi * 2 + y_lo), z: 8, core: 2. Of those that a mesh axis runs over, the one named last changes fastest.
Arguments:
- strain: bfloat16 [2048, 8, 15000], P('chan', 'win'), may hold values from -6 to 6
- gaps: int32 [2048, 8], P('chan', 'win'), may hold values 0 or 1
- source_block: int32 [1], replicated, may hold values from 0 to 32767
Outputs:
- stacks: float32 [64, 2048, 256], P('win', 'chan')
Inputs may be any that keep to these rules, and one draw needn't show every extreme that they name: The plan's step number; the block of 64 channels used as virtual sources is source_block[0] mod 32. `gaps`: 1 where a channel's segment is usable, 0 where it holds a gap or glitch.
All inputs are finite; a program needn't handle non-finite values. No bound on the sum of `gaps` on one device may be relied on, other than what follows from the above.
Results may differ from a plain program's by a relative error of at most 0.01.
Values may be sent and summed in bfloat16 or wider, within the bound.
No kernel may reach another device: no remote copies, remote signals or barrier semaphores. Data moves between devices by JAX's collectives and lax.ppermute only.
A program may use at most 64 MiB of HBM per device.

v0:
```python
import math

import jax
import jax.numpy as jnp
from jax import lax
from jax.sharding import PartitionSpec as P

SAMPLES = 15000
NB = 1280
LAGS = 256
SRC = 64


outer_len = 125
inner_len = 120


def broadcast(block, axis, source):
    block = jnp.where(lax.axis_index(axis) == source, block, jnp.zeros_like(block))
    return lax.psum(block, axis)


def band_spectra(strain, gaps):
    channels, segments, samples = strain.shape
    count = channels * segments
    high = lax.Precision.HIGHEST
    signal = strain.reshape(count, outer_len, inner_len).astype(jnp.float32)
    outer_index = jnp.arange(outer_len, dtype=jnp.int32)
    inner_index = jnp.arange(inner_len, dtype=jnp.int32)
    outer_phase = (outer_index[:, None] * outer_index[None, :] % outer_len).astype(jnp.float32) * (
        2.0 * math.pi / outer_len
    )
    first_real = jnp.einsum("rab,ak->rkb", signal, jnp.cos(outer_phase), precision=high)
    first_imag = -jnp.einsum("rab,ak->rkb", signal, jnp.sin(outer_phase), precision=high)
    twist_phase = (outer_index[:, None] * inner_index[None, :] % samples).astype(jnp.float32) * (
        2.0 * math.pi / samples
    )
    twist_cos = jnp.cos(twist_phase)
    twist_sin = jnp.sin(twist_phase)
    second_real = first_real * twist_cos + first_imag * twist_sin
    second_imag = first_imag * twist_cos - first_real * twist_sin
    kept = -(-(NB + 64) // outer_len)
    upper_index = jnp.arange(kept, dtype=jnp.int32)
    last_phase = (inner_index[:, None] * upper_index[None, :] % inner_len).astype(jnp.float32) * (
        2.0 * math.pi / inner_len
    )
    last_cos = jnp.cos(last_phase)
    last_sin = jnp.sin(last_phase)
    spectrum_real = jnp.einsum("rkb,bj->rjk", second_real, last_cos, precision=high) + jnp.einsum(
        "rkb,bj->rjk", second_imag, last_sin, precision=high
    )
    spectrum_imag = jnp.einsum("rkb,bj->rjk", second_imag, last_cos, precision=high) - jnp.einsum(
        "rkb,bj->rjk", second_real, last_sin, precision=high
    )
    spectrum_real = spectrum_real.reshape(count, kept * outer_len)[:, : NB + 64]
    spectrum_imag = spectrum_imag.reshape(count, kept * outer_len)[:, : NB + 64]
    magnitude = jnp.sqrt(spectrum_real * spectrum_real + spectrum_imag * spectrum_imag)
    level = (
        lax.reduce_window(
            magnitude, jnp.zeros((), magnitude.dtype), lax.add, (1, 65), (1, 1), "VALID"
        )
        / 65.0
    )
    factor = gaps.reshape(count).astype(jnp.float32)[:, None] / (level + 1e-06)
    real_part = (spectrum_real[:, 32 : 32 + NB] * factor).astype(jnp.bfloat16)
    imag_part = (spectrum_imag[:, 32 : 32 + NB] * factor).astype(jnp.bfloat16)
    return jnp.stack([real_part, imag_part]).reshape(2, channels, segments, NB)


def lag_table():
    frequency = 32 + jnp.arange(NB, dtype=jnp.int32)
    offset = jnp.arange(LAGS, dtype=jnp.int32) - LAGS // 2 + SAMPLES
    phase = (frequency[:, None] * offset[None, :] % SAMPLES).astype(jnp.float32) * (
        2.0 * math.pi / SAMPLES
    )
    return jnp.concatenate([jnp.cos(phase), -jnp.sin(phase)], axis=0).astype(jnp.bfloat16)


def lag_term(mine, theirs, table, scale):
    mine_wide = mine.astype(jnp.float32)
    theirs_wide = theirs.astype(jnp.float32)
    high = lax.Precision.HIGHEST
    real_part = jnp.einsum(
        "rgf,sgf->srf", mine_wide[0], theirs_wide[0], precision=high
    ) + jnp.einsum("rgf,sgf->srf", mine_wide[1], theirs_wide[1], precision=high)
    imag_part = jnp.einsum(
        "rgf,sgf->srf", mine_wide[1], theirs_wide[0], precision=high
    ) - jnp.einsum("rgf,sgf->srf", mine_wide[0], theirs_wide[1], precision=high)
    cross = jnp.concatenate([real_part, imag_part], axis=-1).astype(jnp.bfloat16)
    count_src, count_rec = (cross.shape[0], cross.shape[1])
    lagged = jnp.dot(
        cross.reshape(count_src * count_rec, 2 * NB), table, preferred_element_type=jnp.float32
    )
    return lagged.reshape(count_src, count_rec, LAGS) * scale


def local(strain, gaps, source_block):
    receivers, segments = (strain.shape[0], strain.shape[1])
    own_spectra = band_spectra(strain, gaps)
    owners = SRC // receivers
    block_count = lax.axis_size("chan") * receivers // SRC
    block = source_block[0] % block_count
    pieces = []
    for member in range(owners):
        pieces.append(broadcast(own_spectra, "chan", block * owners + member))
    sources = jnp.concatenate(pieces, axis=1)
    table = lag_table()
    windows = lax.axis_size("win")
    scale = 1.0 / math.sqrt(NB * segments * windows)
    return lax.psum_scatter(
        lag_term(own_spectra, sources, table, scale), "win", scatter_dimension=0, tiled=True
    )


def solution(mesh):
    in_specs = (P("chan", "win", None), P("chan", "win"), P())
    out_specs = P("win", "chan", None)
    return jax.shard_map(local, mesh=mesh, in_specs=in_specs, out_specs=out_specs, check_vma=False)
```

profile of v0, /device:TPU:1, one launch (start us, length us, event | category | flops | bytes accessed | tf_op | source)
XLA Modules:
  0.0 635.4 jit_solution(944704871976845501)
XLA Ops:
  6.5 0.0 all-reduce.3.cloned.1.call-start
  7.2 0.3 fusion.55
  7.5 3.9 reshape.153
  11.4 0.9 copy.6
  12.3 1.2 fusion.42
  13.5 1.2 fusion.44
  14.7 0.0 copy-start
  14.7 1.4 fusion.6
  16.1 0.0 copy-done
  16.1 0.0 copy-start.1
  16.1 1.3 fusion.8
  17.5 0.0 copy-done.1
  17.5 2.9 fusion.33
  20.4 0.1 reshape.155
  20.5 2.9 fusion.27
  23.4 0.1 reshape.154
  23.5 0.1 fusion.37
  23.6 11.6 %reduce_window.7 = f32[32,1280]{1,0:T(8,128)S(1)} reduce-window(f32[32,1344]{1,0:T(8,128)S(1)} %fusion.37, f32[]{:T(128)} %constant.79.clone.1), window={size=1x65}, to_apply=%region_0.1 | reduce-window | flops 2621440 | bytes 335876 | tf_op jit(solution)/shard_map/reduce_window | solution.py:59
  35.2 0.2 convert_bitcast_fusion.3
  35.3 0.8 broadcast_select_fusion
  36.1 0.0 all-reduce.3.cloned.1.call-update
  36.1 0.0 reduce-scatter.2.cloned.1.call-start
  36.2 6.2 cosine_convert_fusion
  42.4 520.7 %all-reduce.3.cloned.1.call-done = (bf16[2,32,1,1280]{3,1,2,0:T(8,128)(2,1)}, bf16[2,32,1,1280]{3,1,2,0:T(8,128)(2,1)}) async-done(((bf16[2,32,1,1280]{3,1,2,0:T(8,128)(2,1)}, bf16[2,32,1,1280]{3,1,2,0:T(8,128)(2,1)}), (bf16[2,32,1,1280]{3,1,2,0:T(8,128)(2,1)}, bf16[2,32,1,1280]{3,1,2,0:T(8,128)(2,1)})) %all-reduce.3.cloned.1.call-update) | async-done | bytes 327696 | tf_op jit(solution)/shard_map/psum | solution.py:20
  563.1 0.9 constant_dynamic-update-slice_fusion.1
  564.0 0.9 constant_dynamic-update-slice_fusion
  565.0 3.7 fusion.4
  568.7 4.2 fusion.14
  573.0 0.0 reduce-scatter.2.cloned.1.call-update
  573.0 55.6 %reduce-scatter.2.cloned.1.call-done = f32[8,32,256]{2,1,0:T(8,128)} async-done(((f32[64,32,256]{2,1,0:T(8,128)}), f32[8,32,256]{2,1,0:T(8,128)}) %reduce-scatter.2.cloned.1.call-update) | async-done | bytes 262160 | tf_op jit(solution)/shard_map/reduce_scatter | solution.py:110
  (4 shorter events, 0.1 us)
Async XLA Ops:
  6.5 556.6 %all-reduce.3.cloned.1.call-start = ((), (), s32[]{:S(2)}) async-start(), calls=%async_computation.2 | async-start | bytes 655360 | tf_op jit(solution)/shard_map/psum | solution.py:20
  14.7 1.4 copy-start
  16.1 1.4 copy-start.1
  36.1 592.5 %reduce-scatter.2.cloned.1.call-start = ((), (), s32[]{:S(2)}) async-start(), calls=%async_computation.1 | async-start | bytes 2359296 | tf_op jit(solution)/shard_map/reduce_scatter | solution.py:110
Sparse Core Ops, SparseCore 0:
  36.2 526.8 all-reduce.2
  573.1 55.4 reduce-scatter.1
where the time goes:
time: 636 us; the launch traced here: 635 us
  waiting for transfers between devices  576 us (91%)
  other arithmetic  22.8 us (4%)
  matrix products  15.1 us (2%)
  between operations  14.2 us (2%)
  local copies, waits for them, and re-layouts  6.91 us (1%)
    psum x1, waiting for transfers between devices, broadcast(): return lax.psum(block, axis)  521 us
    reduce_scatter x1, waiting for transfers between devices, local(): lax.psum_scatter(lag_term(own_spectra, sources, table, scale), 'win', sca...  55.6 us
  transfers between devices with their start and end apart: 2, of which 2 were waited for; matrix products, arithmetic and copies ran while one was open for 1% of the time, Pallas kernels for 0%

commit v1 on v0

v1 whole, which is shorter than its diff:
```python
import math

import jax
import jax.numpy as jnp
import numpy as np
from jax import lax
from jax.experimental import pallas as pl
from jax.experimental.pallas import tpu as pltpu
from jax.sharding import Mesh
from jax.sharding import PartitionSpec as P

SAMPLES = 15000
NB = 1280
LAGS = 256
SRC = 64
RADIX = 12
PART = SAMPLES // RADIX
PART_PAD = 1280
BINS = 112
LANES = 128
HALF_ROOT3 = math.sqrt(3.0) / 2.0

F32 = jnp.float32
BF16 = jnp.bfloat16


def piece_count(start):
    return (NB - 1 - start) // RADIX + 1


OFFSETS = [sum(piece_count(s) for s in range(start)) for start in range(RADIX + 1)]


def frequency_order():
    return np.concatenate([start + RADIX * np.arange(piece_count(start)) for start in range(RADIX)])


def transform_tables():
    sample = np.arange(PART_PAD)
    residue = np.arange(RADIX)
    angle = 2.0 * np.pi * ((residue[:, None] * sample[None, :]) % SAMPLES) / SAMPLES
    twiddle = np.stack([np.cos(angle), np.sin(angle)], axis=1).reshape(2 * RADIX, PART_PAD)
    upper = np.arange(BINS)
    angle = 2.0 * np.pi * ((sample[:, None] * upper[None, :]) % PART) / PART
    keep = (sample < PART)[:, None]
    full = np.zeros((PART_PAD, 2 * LANES))
    full[:, :BINS] = np.cos(angle) * keep
    full[:, LANES : LANES + BINS] = np.sin(angle) * keep
    high = full.astype(np.float32).astype(BF16)
    low = (full - high.astype(np.float64)).astype(np.float32).astype(BF16)
    return twiddle.astype(np.float32), high, low


def lag_table():
    frequency = 32 + frequency_order()
    offset = np.arange(LAGS) - LAGS // 2 + SAMPLES
    phase = 2.0 * np.pi * ((frequency[:, None] * offset[None, :]) % SAMPLES) / SAMPLES
    blocks = NB // LANES
    real = np.cos(phase).reshape(blocks, 1, LANES, LAGS)
    imag = -np.sin(phase).reshape(blocks, 1, LANES, LAGS)
    table = np.concatenate([real, imag], axis=1).reshape(2 * NB, LAGS)
    return table.astype(np.float32).astype(BF16)


def real_radix12(x):
    even = [None] + [x[q] + x[RADIX - q] for q in range(1, 6)]
    odd = [None] + [x[q] - x[RADIX - q] for q in range(1, 6)]
    sum06, dif06 = x[0] + x[6], x[0] - x[6]
    e15p, e15m, e24p, e24m = even[1] + even[5], even[1] - even[5], even[2] + even[4], even[2] - even[4]
    o15p, o15m, o24p, o24m = odd[1] + odd[5], odd[1] - odd[5], odd[2] + odd[4], odd[2] - odd[4]
    c, h = HALF_ROOT3, 0.5
    real = [
        sum06 + e15p + e24p + even[3],
        dif06 + c * e15m + h * e24m,
        sum06 + h * (e15p - e24p) - even[3],
        dif06 - e24m,
        sum06 - h * (e15p + e24p) + even[3],
        dif06 - c * e15m + h * e24m,
        sum06 - e15p + e24p - even[3],
    ]
    imag = [
        None,
        -(h * o15p + c * o24p + odd[3]),
        -c * (o15m + o24m),
        odd[3] - o15p,
        -c * (o15m - o24m),
        c * o24p - h * o15p - odd[3],
        None,
    ]
    return real, imag


def row_of(residue, part):
    return 0 if residue == 0 else 32 * (2 * residue - 1 + part)


def roll(value, shift, axis):
    size = value.shape[axis]
    shift = shift % size
    return value if shift == 0 else pltpu.roll(value, shift, axis)


def spectra_kernel(x_ref, gaps_ref, tw_ref, high_ref, low_ref, w_ref, s_ref, tail, a_ref, p_ref):
    blocks = PART_PAD // LANES
    last = SAMPLES // LANES * LANES
    lane16 = lax.broadcasted_iota(jnp.int32, (16, LANES), 1)
    tail[...] = jnp.zeros_like(tail)
    tail[:, : SAMPLES - last] = x_ref[:, last:].astype(F32)

    for half in range(2):
        rows = slice(16 * half, 16 * half + 16)
        held = {}

        def shifted(q, place):
            if (q, place) not in held:
                start = (q * PART // LANES + place) * LANES
                if start >= last:
                    raw = tail[rows, :]
                else:
                    raw = x_ref[rows, start : start + LANES].astype(F32)
                held[(q, place)] = roll(raw, -(q * PART % LANES), 1)
            return held[(q, place)]

        for block in range(blocks):
            parts = []
            for q in range(RADIX):
                turn = q * PART % LANES
                now = shifted(q, block)
                if turn and not (q == RADIX - 1 and block == blocks - 1):
                    now = jnp.where(lane16 < LANES - turn, now, shifted(q, block + 1))
                elif turn:
                    now = jnp.where(lane16 < LANES - turn, now, shifted(q, block + 1))
                parts.append(now)
            real, imag = real_radix12(parts)
            columns = slice(LANES * block, LANES * (block + 1))
            wide = slice(PART_PAD + LANES * block, PART_PAD + LANES * (block + 1))

            def keep(value, residue, part):
                at = row_of(residue, part) + 16 * half
                high = value.astype(BF16)
                a_ref[at : at + 16, columns] = high
                a_ref[at : at + 16, wide] = (value - high.astype(F32)).astype(BF16)

            keep(real[0], 0, 0)
            for residue in range(1, RADIX):
                base = min(residue, RADIX - residue)
                re, im = real[base], imag[base]
                cosine = tw_ref[2 * residue : 2 * residue + 1, columns]
                sine = tw_ref[2 * residue + 1 : 2 * residue + 2, columns]
                if im is None:
                    keep(re * cosine, residue, 0)
                    keep(-(re * sine), residue, 1)
                elif residue < 6:
                    keep(re * cosine + im * sine, residue, 0)
                    keep(im * cosine - re * sine, residue, 1)
                else:
                    keep(re * cosine - im * sine, residue, 0)
                    keep(-(im * cosine) - re * sine, residue, 1)

    p_ref[...] = (
        jnp.dot(a_ref[:, :PART_PAD], high_ref[...], preferred_element_type=F32)
        + jnp.dot(a_ref[:, PART_PAD:], high_ref[...], preferred_element_type=F32)
        + jnp.dot(a_ref[:, :PART_PAD], low_ref[...], preferred_element_type=F32)
    )

    lane = lax.broadcasted_iota(jnp.int32, (8, LANES), 1)
    row = lax.broadcasted_iota(jnp.int32, (8, LANES), 0)
    flat = []
    for group in range(4):
        first = 8 * group
        re, im, mag = [], [], []
        for residue in range(RADIX):
            at = row_of(residue, 0) + first
            real = p_ref[at : at + 8, :LANES]
            imag = -p_ref[at : at + 8, LANES:]
            if residue:
                other = row_of(residue, 1) + first
                real = real + p_ref[other : other + 8, LANES:]
                imag = imag + p_ref[other : other + 8, :LANES]
            re.append(real)
            im.append(imag)
            mag.append(jnp.sqrt(real * real + imag * imag))
        five, five_next, sixth, sixth_next = [], [], [], []
        for residue in range(RADIX):
            m = mag[residue]
            two = m + roll(m, -1, 1)
            four = two + roll(two, -2, 1)
            total = four + roll(m, -4, 1)
            five.append(total)
            five_next.append(roll(total, -1, 1))
            sixth.append(roll(m, -5, 1))
            sixth_next.append(roll(m, -6, 1) if residue < 4 else None)
        after = [None] * (RADIX + 1)
        for start in range(RADIX - 1, -1, -1):
            after[start] = five[start] if after[start + 1] is None else after[start + 1] + five[start]
        gap = gaps_ref[first : first + 8, :].astype(F32)
        before = None
        out = [[None] * (NB // LANES), [None] * (NB // LANES)]
        for start in range(RADIX):
            level = after[start] if before is None else after[start] + before
            for extra in range(start, start + 5):
                level = level + (sixth[extra] if extra < RADIX else sixth_next[extra - RADIX])
            before = five_next[start] if before is None else before + five_next[start]
            factor = gap / (level / 65.0 + 1e-06)
            residue = start - 4 if start >= 4 else start + 8
            shift = 3 if start >= 4 else 2
            factor = roll(factor, shift, 1)
            offset = OFFSETS[start]
            end = OFFSETS[start + 1]
            for part, spectrum in enumerate((re, im)):
                piece = roll(spectrum[residue] * factor, offset - shift, 1)
                for block in range(offset // LANES, (end - 1) // LANES + 1):
                    low = max(offset - block * LANES, 0)
                    if out[part][block] is None:
                        out[part][block] = piece
                    else:
                        out[part][block] = jnp.where(lane >= low, piece, out[part][block])
        flat.append(out[0] + out[1])

    columns = 2 * NB // LANES
    for block in range(columns):
        for half in range(2):
            pair = jnp.concatenate([flat[2 * half][block], flat[2 * half + 1][block]], axis=0)
            w_ref[16 * half : 16 * half + 16, LANES * block : LANES * (block + 1)] = pair.astype(BF16)
    each = columns // 4
    for member in range(4):
        mixed = []
        for block in range(columns):
            value = None
            for group in range(4):
                turned = roll(flat[group][block], 2 * group - 2 * member, 0)
                value = turned if value is None else jnp.where(row >= 2 * group, turned, value)
            mixed.append(value)
        for pair in range(2):
            at = 32 * member + 16 * pair
            for block in range(each):
                both = jnp.concatenate([mixed[2 * pair * each + block], mixed[(2 * pair + 1) * each + block]], axis=0)
                s_ref[at : at + 16, LANES * block : LANES * (block + 1)] = both.astype(BF16)


def spectra(strain, gaps):
    twiddle, high, low = transform_tables()
    return pl.pallas_call(
        spectra_kernel,
        out_shape=(
            jax.ShapeDtypeStruct((32, 2 * NB), BF16),
            jax.ShapeDtypeStruct((128, 640), BF16),
        ),
        scratch_shapes=[
            pltpu.VMEM((32, LANES), F32),
            pltpu.VMEM((23 * 32, 2 * PART_PAD), BF16),
            pltpu.VMEM((23 * 32, 2 * LANES), F32),
        ],
        compiler_params=pltpu.CompilerParams(vmem_limit_bytes=40 * 1024 * 1024),
        name="spectra",
    )(strain, gaps, jnp.asarray(twiddle), jnp.asarray(high), jnp.asarray(low))


def tree_sum(terms):
    while len(terms) > 1:
        terms = [terms[i] + terms[i + 1] for i in range(0, len(terms), 2)]
    return terms[0]


def stack_kernel(r_ref, src_ref, tab_ref, out_ref, wide, cross):
    wide[...] = src_ref[...].astype(F32)
    scale = 1.0 / math.sqrt(NB * 8)
    total = None
    for block in range(NB // LANES):
        half, inner = block // 5, block % 5
        columns = slice(LANES * inner, LANES * (inner + 1))
        real = [r_ref[32 * w : 32 * w + 32, LANES * block : LANES * (block + 1)] for w in range(8)]
        imag = [r_ref[32 * w : 32 * w + 32, NB + LANES * block : NB + LANES * (block + 1)] for w in range(8)]
        for source in range(8):
            member, e = source // 2, source % 2
            re_terms, im_terms = [], []
            for w in range(8):
                at_re = (member * 4 + half) * 16 + 2 * w + e
                at_im = (member * 4 + 2 + half) * 16 + 2 * w + e
                s_re = jnp.broadcast_to(wide[at_re : at_re + 1, columns], (32, LANES)).astype(BF16)
                s_im = jnp.broadcast_to(wide[at_im : at_im + 1, columns], (32, LANES)).astype(BF16)
                re_terms.append(real[w] * s_re + imag[w] * s_im)
                im_terms.append(imag[w] * s_re - real[w] * s_im)
            rows = slice(32 * source, 32 * source + 32)
            cross[rows, 2 * LANES * block : 2 * LANES * block + LANES] = tree_sum(re_terms)
            cross[rows, 2 * LANES * block + LANES : 2 * LANES * (block + 1)] = tree_sum(im_terms)
    out_ref[...] = jnp.dot(cross[...], tab_ref[...], preferred_element_type=F32) * scale


def stacked(receivers, sources):
    return pl.pallas_call(
        stack_kernel,
        out_shape=jax.ShapeDtypeStruct((256, LAGS), F32),
        scratch_shapes=[
            pltpu.VMEM((256, 640), F32),
            pltpu.VMEM((256, 2 * NB), BF16),
        ],
        compiler_params=pltpu.CompilerParams(vmem_limit_bytes=40 * 1024 * 1024),
        name="stack",
    )(receivers, sources, jnp.asarray(lag_table()))


def local(strain, gaps, source_block):
    block = source_block[0] % 32
    root_y, root_z = block // 8, block % 8
    whitened, scattered = spectra(strain.reshape(32, SAMPLES), gaps)
    receivers = lax.all_gather(whitened, ("x", "yl"), tiled=True)
    with jax.named_scope("scatter"):
        got = lax.all_to_all(scattered.reshape(16, 8, 640), ("z", "co"), 0, 0)
    mine = lax.dynamic_slice(got, (2 * root_z, 0, 0), (2, 8, 640)).reshape(8, 2, 640)
    with jax.named_scope("exchange"):
        sent = jnp.broadcast_to(mine[None], (4, 8, 2, 640)).reshape(32, 2, 640)
        got = lax.all_to_all(sent, ("yh", "x", "yl"), 0, 0)
    mine = lax.dynamic_slice(got, (8 * root_y, 0, 0), (8, 2, 640)).reshape(16, 640)
    with jax.named_scope("gather"):
        sent = jnp.broadcast_to(mine[None], (16, 16, 640))
        sources = lax.all_to_all(sent, ("z", "co"), 0, 0)
    return stacked(receivers, sources.reshape(256, 640)).reshape(8, 32, LAGS)


def solution(mesh):
    split = Mesh(mesh.devices.reshape(4, 8, 2, 4, 2), ("yh", "z", "co", "x", "yl"))
    chan, win = ("yh", "z", "co"), ("x", "yl")
    in_specs = (P(chan, win, None), P(chan, win), P())
    out_specs = P(win, chan, None)
    return jax.shard_map(local, mesh=split, in_specs=in_specs, out_specs=out_specs, check_vma=False)
```

time: 636 us -> 87.5 us (0.14)
  waiting for transfers between devices: 576 us -> 19.3 us
  other arithmetic: 22.8 us -> 0 us
  starting transfers between devices: 0.04 us -> 21.6 us
  blocking collectives: 0 us -> 16.6 us
  matrix products: 15.1 us -> 0 us
  Pallas kernels: 0 us -> 8.23 us
    psum x1 -> x0, waiting for transfers between devices: 521 us -> none  [broadcast(): return lax.psum(block, axis)]
    reduce_scatter x1 -> x0, waiting for transfers between devices: 55.6 us -> none  [local(): lax.psum_scatter(lag_term(own_spectra, sources, table, scale), 'win', sca...]
    all_to_all x0 -> x2, starting transfers between devices: none -> 21.6 us  [the longest x1 12 us: local(): got = lax.all_to_all(scattered.reshape(16, 8, 640), ('z', 'co'), 0, 0)]
    all_to_all x0 -> x2, waiting for transfers between devices: none -> 19.3 us  [the longest x1 10.3 us: local(): got = lax.all_to_all(sent, ('yh', 'x', 'yl'), 0, 0)]
    another operation x4 -> x0, other arithmetic: 18 us -> none  [the longest x1 11.6 us: band_spectra(): lax.reduce_window(magnitude, jnp.zeros((), magnitude.dtype), lax.add, (1,...]
    all_to_all x0 -> x1, blocking collectives: none -> 16.6 us  [local(): sources = lax.all_to_all(sent, ('z', 'co'), 0, 0)]
    dot_general x5 -> x0, matrix products: 12.7 us -> none  [the longest x1 4.25 us: lag_term(): jnp.dot(cross.reshape(count_src * count_rec, 2 * NB), table, preferred_el...]
    pallas_call x0 -> x2, Pallas kernels: none -> 8.23 us  [the longest x1 4.18 us: spectra(): pl.pallas_call(spectra_kernel, out_shape=(jax.ShapeDtypeStruct((32, 2 * N...]
  transfers between devices with their start and end apart: 2 -> 3, of which waited for: 2 -> 2; matrix products, arithmetic and copies ran while one was open for 1% -> 1% of each run, Pallas kernels for 0% -> 0%
where the time goes in v1:
time: 87.5 us; the launch traced here: 87 us
  starting transfers between devices  21.6 us (25%)
  waiting for transfers between devices  19.3 us (22%)
  blocking collectives  16.6 us (19%)
  between operations  14.1 us (16%)
  Pallas kernels  8.23 us (9%)
  local copies, waits for them, and re-layouts  7.08 us (8%)
    all_to_all x1, blocking collectives, local(): sources = lax.all_to_all(sent, ('z', 'co'), 0, 0)  16.6 us
    all_to_all x1, starting transfers between devices, local(): got = lax.all_to_all(scattered.reshape(16, 8, 640), ('z', 'co'), 0, 0)  12 us
    all_to_all x1, waiting for transfers between devices, local(): got = lax.all_to_all(sent, ('yh', 'x', 'yl'), 0, 0)  10.3 us
    all_to_all x1, starting transfers between devices, local(): got = lax.all_to_all(sent, ('yh', 'x', 'yl'), 0, 0)  9.67 us
    all_to_all x1, waiting for transfers between devices, local(): got = lax.all_to_all(scattered.reshape(16, 8, 640), ('z', 'co'), 0, 0)  8.96 us
    unnamed x13, local copies, waits for them, and re-layouts  6.33 us
    pallas_call x1, Pallas kernels, spectra(): pl.pallas_call(spectra_kernel, out_shape=(jax.ShapeDtypeStruct((32, 2 * N...  4.18 us
    pallas_call x1, Pallas kernels, stacked(): pl.pallas_call(stack_kernel, out_shape=jax.ShapeDtypeStruct((256, LAGS),...  4.05 us
  transfers between devices with their start and end apart: 3, of which 2 were waited for; matrix products, arithmetic and copies ran while one was open for 1% of the time, Pallas kernels for 0%

profile of v1, /device:TPU:1, one launch (start us, length us, event | category | flops | bytes accessed | tf_op | source)
XLA Modules:
  0.0 87.0 jit_solution(561149807203599697)
XLA Ops:
  6.5 0.0 all-gather.2.cloned.1.call-start
  6.5 0.7 copy.8.gaps_ref
  7.3 0.0 copy-start.2
  7.3 1.2 %copy-done.2 = bf16[32,1,15000]{2,0,1:T(8,128)(2,1)S(1)} copy-done((bf16[32,1,15000]{2,0,1:T(8,128)(2,1)S(1)}, bf16[32,1,15000]{2,0,1:T(8,128)(2,1)}, u32[]{:S(2)}) %copy-start.2) | copy-done | bytes 960024
  8.5 0.0 copy-start.3
  8.5 1.1 %copy-done.3 = bf16[1280,256]{1,0:T(8,128)(2,1)S(1)} copy-done((bf16[1280,256]{1,0:T(8,128)(2,1)S(1)}, bf16[1280,256]{1,0:T(8,128)(2,1)}, u32[]{:S(2)}) %copy-start.3) | copy-done | bytes 655384
  9.6 0.0 copy-start.4
  9.6 1.1 %copy-done.4 = bf16[1280,256]{1,0:T(8,128)(2,1)S(1)} copy-done((bf16[1280,256]{1,0:T(8,128)(2,1)S(1)}, bf16[1280,256]{1,0:T(8,128)(2,1)}, u32[]{:S(2)}) %copy-start.4) | copy-done | bytes 655384
  10.6 0.0 copy-start.5
  10.6 0.9 %copy-done.5 = f32[24,1280]{1,0:T(8,128)S(1)} copy-done((f32[24,1280]{1,0:T(8,128)S(1)}, f32[24,1280]{1,0:T(8,128)}, u32[]{:S(2)}) %copy-start.5) | copy-done | bytes 122904
  11.5 4.2 %spectra.1 = (bf16[32,2560]{1,0:T(8,128)(2,1)}, bf16[128,640]{1,0:T(8,128)(2,1)}) custom-call(bf16[32,15000]{1,0:T(8,128)(2,1)S(1)} %bitcast.10, s32[32,1]{1,0:T(8,128)S(1)} %copy.8.gaps_ref, f32[24,1280]{1,0:T(8,128)S(1)} %copy-done.5, bf16[1280,256]{1,0:T(8,128)(2,1)S(1)} %copy-done.3, bf16[1280,256]{1,0:T(8,128)(2,1)S(1)} %copy-done.4), custom_call_target="tpu_custom_call" | custom-call | tf_op jit(solution)/shard_map/spectra/pallas_call | solution.py:243
  15.7 0.0 copy-start
  15.7 0.0 all-gather.2.cloned.1.call-update
  15.8 12.0 %all-to-all-start = ((bf16[16,8,640]{2,1,0:T(8,128)(2,1)}), bf16[16,8,640]{2,1,0:T(8,128)(2,1)S(1)}, u32[]{:S(2)}, u32[]{:S(2)}) async-start(bf16[16,8,640]{2,1,0:T(8,128)(2,1)} %bitcast.1), calls=%async_computation | async-start | bytes 327680 | tf_op jit(solution)/shard_map/scatter/all_to_all | solution.py:309
  28.4 9.0 %all-to-all-done = bf16[16,8,640]{2,1,0:T(8,128)(2,1)S(1)} async-done(((bf16[16,8,640]{2,1,0:T(8,128)(2,1)}), bf16[16,8,640]{2,1,0:T(8,128)(2,1)S(1)}, u32[]{:S(2)}, u32[]{:S(2)}) %all-to-all-start) | async-done | bytes 163872 | tf_op jit(solution)/shard_map/scatter/all_to_all | solution.py:309
  37.4 0.7 broadcast_in_dim.15
  38.1 9.7 %all-to-all-start.1 = ((bf16[32,2,640]{2,1,0:T(2,128)(2,1)}), bf16[32,2,640]{2,1,0:T(2,128)(2,1)S(1)}, u32[]{:S(2)}, u32[]{:S(2)}) async-start(bf16[32,2,640]{2,1,0:T(2,128)(2,1)} %bitcast.3), calls=%async_computation.1 | async-start | bytes 163840 | tf_op jit(solution)/shard_map/exchange/all_to_all | solution.py:313
  47.8 10.3 %all-to-all-done.1 = bf16[32,2,640]{2,1,0:T(2,128)(2,1)S(1)} async-done(((bf16[32,2,640]{2,1,0:T(2,128)(2,1)}), bf16[32,2,640]{2,1,0:T(2,128)(2,1)S(1)}, u32[]{:S(2)}, u32[]{:S(2)}) %all-to-all-start.1) | async-done | bytes 81952 | tf_op jit(solution)/shard_map/exchange/all_to_all | solution.py:313
  58.2 16.6 %all_to_all.15 = bf16[16,16,640]{2,1,0:T(8,128)(2,1)S(1)} all-to-all(bf16[16,16,640]{2,1,0:T(8,128)(2,1)S(1)} %broadcast_in_dim.17), channel_id=1, replica_groups=mesh['yh'=4,'z'=8,'co'=2,'x'=4,'yl'=2] {'z','co'}, dimensions={0} | all-to-all | bytes 655360 | tf_op jit(solution)/shard_map/gather/all_to_all | solution.py:317
  74.8 0.0 all-gather.2.cloned.1.call-done.r_ref
  74.8 0.0 copy-done
  74.8 0.0 copy-start.1
  74.8 1.3 %copy-done.1 = bf16[256,2560]{1,0:T(8,128)(2,1)S(1)} copy-done((bf16[256,2560]{1,0:T(8,128)(2,1)S(1)}, bf16[256,2560]{1,0:T(8,128)(2,1)}, u32[]{:S(2)}) %copy-start.1) | copy-done | bytes 1310744
  76.1 4.1 %stack.1 = f32[256,256]{1,0:T(8,128)} custom-call(bf16[256,2560]{1,0:T(8,128)(2,1)S(1)} %copy-done.1, bf16[256,640]{1,0:T(8,128)(2,1)S(1)} %bitcast.9, bf16[2560,256]{1,0:T(8,128)(2,1)S(1)} %copy-done), custom_call_target="tpu_custom_call" | custom-call | tf_op jit(solution)/shard_map/stack/pallas_call | solution.py:291
  (5 shorter events, 0.1 us)
Async XLA Ops:
  6.5 68.3 %all-gather.2.cloned.1.call-start = ((), (), s32[]{:S(2)}) async-start(), calls=%async_computation.3 | async-start | bytes 1474560 | tf_op jit(solution)/shard_map/all_gather | solution.py:307
  7.3 1.2 %copy-start.2 = (bf16[32,1,15000]{2,0,1:T(8,128)(2,1)S(1)}, bf16[32,1,15000]{2,0,1:T(8,128)(2,1)}, u32[]{:S(2)}) copy-start(bf16[32,1,15000]{2,0,1:T(8,128)(2,1)} %param.7) | copy-start | bytes 2880004
  8.5 1.1 %copy-start.3 = (bf16[1280,256]{1,0:T(8,128)(2,1)S(1)}, bf16[1280,256]{1,0:T(8,128)(2,1)}, u32[]{:S(2)}) copy-start(bf16[1280,256]{1,0:T(8,128)(2,1)} %constant.50.clone.high_ref) | copy-start | bytes 1966084
  9.6 1.1 %copy-start.4 = (bf16[1280,256]{1,0:T(8,128)(2,1)S(1)}, bf16[1280,256]{1,0:T(8,128)(2,1)}, u32[]{:S(2)}) copy-start(bf16[1280,256]{1,0:T(8,128)(2,1)} %constant.51.clone.low_ref) | copy-start | bytes 1966084
  10.6 0.9 %copy-start.5 = (f32[24,1280]{1,0:T(8,128)S(1)}, f32[24,1280]{1,0:T(8,128)}, u32[]{:S(2)}) copy-start(f32[24,1280]{1,0:T(8,128)} %constant.49.clone.tw_ref) | copy-start | bytes 368644
  15.7 59.1 %copy-start = (bf16[2560,256]{1,0:T(8,128)(2,1)S(1)}, bf16[2560,256]{1,0:T(8,128)(2,1)}, u32[]{:S(2)}) copy-start(bf16[2560,256]{1,0:T(8,128)(2,1)} %constant.52.clone.tab_ref) | copy-start | bytes 3932164
  15.8 21.6 %all-to-all-start = ((bf16[16,8,640]{2,1,0:T(8,128)(2,1)}), bf16[16,8,640]{2,1,0:T(8,128)(2,1)S(1)}, u32[]{:S(2)}, u32[]{:S(2)}) async-start(bf16[16,8,640]{2,1,0:T(8,128)(2,1)} %bitcast.1), calls=%async_computation | async-start | bytes 327680 | tf_op jit(solution)/shard_map/scatter/all_to_all | solution.py:309
  38.1 20.0 %all-to-all-start.1 = ((bf16[32,2,640]{2,1,0:T(2,128)(2,1)}), bf16[32,2,640]{2,1,0:T(2,128)(2,1)S(1)}, u32[]{:S(2)}, u32[]{:S(2)}) async-start(bf16[32,2,640]{2,1,0:T(2,128)(2,1)} %bitcast.3), calls=%async_computation.1 | async-start | bytes 163840 | tf_op jit(solution)/shard_map/exchange/all_to_all | solution.py:313
  74.8 1.3 %copy-start.1 = (bf16[256,2560]{1,0:T(8,128)(2,1)S(1)}, bf16[256,2560]{1,0:T(8,128)(2,1)}, u32[]{:S(2)}) copy-start(bf16[256,2560]{1,0:T(8,128)(2,1)} %all-gather.2.cloned.1.call-done.r_ref) | copy-start | bytes 3932164
Sparse Core Ops, SparseCore 0:
  15.9 49.5 all-gather.1
